TPU v7x, 32 devices: a whole 2x2x4 slice. The times are simulated.
32 devices in a mesh: vertex: 8 (over z, core), tm: 4 (over y, x).
Axes of the slice: x: 2, y: 2, z: 4, core: 2. Of those that a mesh axis runs over, the one named last changes fastest.
Arguments:
- features: bfloat16 [4, 8192, 512], P('tm', 'vertex'), may hold values from -6 to 6
- tile_coord: int32 [4, 1024, 2], P('tm', 'vertex'), may hold values from 0 to 63, as said below
- tile_count: int32 [4, 8], P('tm', 'vertex'), may hold values from 1 to 128, as said below
- tile_values: bfloat16 [4, 1024, 128, 128], P('tm', 'vertex'), may hold values from -0.125 to 0.125
- w_agg: bfloat16 [512, 512], replicated, may hold values from -0.25 to 0.25
- w_root: bfloat16 [512, 512], replicated, may hold values from -0.25 to 0.25
- time_embed: bfloat16 [4, 512], replicated, may hold values from -6 to 6
- gain_first: bfloat16 [512], replicated, may hold values from 0.25 to 1.75
- w_qkv: bfloat16 [512, 1536], replicated, may hold values from -12 to 12
- w_out: bfloat16 [512, 512], replicated, may hold values from -0.25 to 0.25
- gain_second: bfloat16 [512], replicated, may hold values from 0.25 to 1.75
- w_up: bfloat16 [512, 1024], replicated, may hold values from -0.25 to 0.25
- w_down: bfloat16 [1024, 512], replicated, may hold values from -0.1875 to 0.1875
Outputs:
- layer_out: bfloat16 [4, 8192, 512], P(None, ('vertex', 'tm'))
Inputs may be any that keep to these rules, and one draw needn't show every extreme that they name: `tile_coord`: entry 0 of a slot is a row block 0 to 7 of the device's own vertices, entry 1 a column block 0 to 63; no pair repeats among one device's 128 slots, live or not. `tile_count`: live slots are the first ones of a device; in every snapshot some device has all 128 slots live.
All inputs are finite; a program needn't handle non-finite values.
Results may differ from a plain program's by a relative error of at most 0.006.
Values may be sent and summed in bfloat16 or wider, within the bound.
A program may use at most 192 MiB of HBM per device.

v0:
```python
import functools
import math

import jax
import jax.numpy as jnp
from jax import lax
from jax.experimental import pallas as pl
from jax.experimental.pallas import tpu as pltpu
from jax.sharding import PartitionSpec as P

HEADS = 8
CORES = 2
MESH = pl.DeviceIdType.MESH
MIB = 1 << 20


def graph_kernel(
    cfg,
    table_ref,
    feat_ref,
    tiles_ref,
    wagg_ref,
    wroot_ref,
    land_ref,
    xbuf,
    tiles_v,
    wagg_v,
    wroot_v,
    acc,
    a_buf,
    stage,
    local_sem,
    send_sem,
    recv_sem,
    a2a_send,
    a2a_recv,
):
    n_vertex, n_tm, chunks, chunk, tile, slots = cfg
    chips = n_vertex // CORES
    local = feat_ref.shape[0]
    row_blocks = local // tile
    col_blocks = n_vertex * row_blocks
    per_chunk = chunk // tile
    item = local // n_tm
    me = lax.axis_index("vertex")
    tm = lax.axis_index("tm")
    z = me // CORES
    core = me % CORES
    sibling = z * CORES + (1 - core)
    has_right = z < chips - 1
    has_left = z > 0

    barrier = pltpu.get_barrier_semaphore()

    def greet(ids):
        pl.semaphore_signal(barrier, inc=1, device_id=ids, device_id_type=MESH)

    greet({"vertex": sibling})

    @pl.when(has_right)
    def _():
        greet({"vertex": me + CORES})

    @pl.when(has_left)
    def _():
        greet({"vertex": me - CORES})

    for i in range(1, n_tm):
        greet({"tm": lax.rem(tm + i, n_tm)})

    own_copy = pltpu.make_async_copy(feat_ref, xbuf.at[me], local_sem.at[0])
    tile_copy = pltpu.make_async_copy(tiles_ref, tiles_v.at[pl.ds(0, slots)], local_sem.at[1])
    agg_copy = pltpu.make_async_copy(wagg_ref, wagg_v, local_sem.at[2])
    root_copy = pltpu.make_async_copy(wroot_ref, wroot_v, local_sem.at[3])
    own_copy.start()
    tile_copy.start()
    agg_copy.start()
    root_copy.start()

    ends = jnp.where(has_right, 1, 0) + jnp.where(has_left, 1, 0)
    pl.semaphore_wait(barrier, n_tm + ends)

    def piece(shard, part, way, target):
        rows = pl.ds(pl.multiple_of(part * chunk, chunk), chunk)
        return pltpu.make_async_remote_copy(
            src_ref=xbuf.at[shard, rows],
            dst_ref=xbuf.at[shard, rows],
            send_sem=send_sem.at[way, shard, part],
            recv_sem=recv_sem.at[shard, part],
            device_id={"vertex": target},
            device_id_type=MESH,
        )

    def spread(shard, part, right, left):
        @pl.when(right)
        def _():
            piece(shard, part, 0, me + CORES).start()

        @pl.when(left)
        def _():
            piece(shard, part, 1, me - CORES).start()

        piece(shard, part, 2, sibling).start()

    def settle(shard, part, right, left):
        @pl.when(right)
        def _():
            piece(shard, part, 0, me + CORES).wait_send()

        @pl.when(left)
        def _():
            piece(shard, part, 1, me - CORES).wait_send()

        piece(shard, part, 2, sibling).wait_send()

    def arrived(shard, part):
        piece(shard, part, 2, sibling).wait_recv()

    def multiply(shard, part):
        first = shard * row_blocks + part * per_chunk
        for r in range(row_blocks):
            for j in range(per_chunk):
                slot = table_ref[r * col_blocks + first + j]
                a_buf[r * tile : (r + 1) * tile, j * tile : (j + 1) * tile] = tiles_v[slot]
        rows = pl.ds(pl.multiple_of(part * chunk, chunk), chunk)
        acc[...] += jnp.dot(a_buf[...], xbuf[shard, rows], preferred_element_type=jnp.float32)

    own_copy.wait()

    def send_own(part, carry):
        spread(me, part, has_right, has_left)
        return carry

    lax.fori_loop(0, chunks, send_own, 0)
    tiles_v[slots] = jnp.zeros(tiles_v.shape[1:], tiles_v.dtype)
    acc[...] = jnp.zeros_like(acc)
    tile_copy.wait()
    agg_copy.wait()
    root_copy.wait()

    def first_step(i, carry):
        part = lax.rem(i, chunks)
        other = i // chunks
        shard = me + other * (sibling - me)

        @pl.when(other == 1)
        def _():
            arrived(shard, part)

        multiply(shard, part)
        return carry

    lax.fori_loop(0, CORES * chunks, first_step, 0)

    def step(i, carry):
        hop = i // chunks + 1
        part = lax.rem(i, chunks)
        low = z - hop
        high = z + hop

        @pl.when(low >= 0)
        def _():
            shard = low * CORES + core
            arrived(shard, part)
            spread(shard, part, has_right, False)

        @pl.when(high < chips)
        def _():
            shard = high * CORES + core
            arrived(shard, part)
            spread(shard, part, False, has_left)

        def use(j, inner):
            side = lax.rem(j, 2)
            other = j // 2
            chip = z - hop + side * 2 * hop
            shard = chip * CORES + core + other * (1 - 2 * core)

            @pl.when(jnp.logical_and(chip >= 0, chip < chips))
            def _():
                @pl.when(other == 1)
                def _():
                    arrived(shard, part)

                multiply(shard, part)

            return inner

        lax.fori_loop(0, 4, use, 0)
        return carry

    lax.fori_loop(0, (chips - 1) * chunks, step, 0)

    def block(i, carry):
        to = lax.rem(tm + i, n_tm)
        rows = pl.ds(pl.multiple_of(to * item, item), item)
        neighbor_sum = acc[rows].astype(jnp.bfloat16)
        combined = jnp.dot(neighbor_sum, wagg_v[...], preferred_element_type=jnp.float32)
        combined += jnp.dot(xbuf[me, rows], wroot_v[...], preferred_element_type=jnp.float32)
        stage[to] = jax.nn.gelu(combined).astype(jnp.bfloat16)

        @pl.when(i < n_tm)
        def _():
            trade(to).start()

        return carry

    def trade(to):
        return pltpu.make_async_remote_copy(
            src_ref=stage.at[to],
            dst_ref=land_ref.at[tm],
            send_sem=a2a_send.at[to],
            recv_sem=a2a_recv.at[tm],
            device_id={"tm": to},
            device_id_type=MESH,
        )

    def landed(source):
        return pltpu.make_async_remote_copy(
            src_ref=stage.at[source],
            dst_ref=land_ref.at[source],
            send_sem=a2a_send.at[source],
            recv_sem=a2a_recv.at[source],
            device_id={"tm": source},
            device_id_type=MESH,
        )

    lax.fori_loop(1, n_tm + 1, block, 0)
    land_ref[tm] = stage[tm]

    def settle_own(part, carry):
        settle(me, part, has_right, has_left)
        return carry

    lax.fori_loop(0, chunks, settle_own, 0)

    def settle_step(i, carry):
        hop = i // chunks + 1
        part = lax.rem(i, chunks)
        low = z - hop
        high = z + hop

        @pl.when(low >= 0)
        def _():
            settle(low * CORES + core, part, has_right, False)

        @pl.when(high < chips)
        def _():
            settle(high * CORES + core, part, False, has_left)

        return carry

    lax.fori_loop(0, (chips - 1) * chunks, settle_step, 0)

    def finish(i, carry):
        partner = lax.rem(tm + i, n_tm)
        trade(partner).wait_send()
        landed(partner).wait_recv()
        return carry

    lax.fori_loop(1, n_tm, finish, 0)


def norm_rows(values, gain):
    scale = lax.rsqrt(jnp.mean(values * values, axis=-1, keepdims=True) + 1e-06)
    return values * scale * gain


def matmul(left, right):
    return jnp.dot(left, right, preferred_element_type=jnp.float32)


def temporal_body(rows_ref, embed_ref, gain1_ref, qkv_ref, wout_ref, gain2_ref, up_ref, down_ref, out_ref):
    snaps, items, width = rows_ref.shape
    head = width // HEADS
    lanes = 128
    size = max(16, min(items, 512 // snaps))
    col_head = lax.broadcasted_iota(jnp.int32, (width, lanes), 0) // head
    gather_heads = (col_head == lax.broadcasted_iota(jnp.int32, (width, lanes), 1)).astype(jnp.bfloat16)
    row_head = lax.broadcasted_iota(jnp.int32, (lanes, width), 1) // head
    widen_heads = (row_head == lax.broadcasted_iota(jnp.int32, (lanes, width), 0)).astype(jnp.bfloat16)

    def body(i, carry):
        at = pl.ds(pl.multiple_of(i * size, size), size)
        embed = embed_ref[...].astype(jnp.float32)
        mixed = jnp.concatenate(
            [rows_ref[t, at].astype(jnp.float32) + embed[t : t + 1] for t in range(snaps)], axis=0
        )
        normed = norm_rows(mixed, gain1_ref[...].astype(jnp.float32)).astype(jnp.bfloat16)
        qkv = matmul(normed, qkv_ref[...]).astype(jnp.bfloat16)
        query = [qkv[t * size : (t + 1) * size, :width].astype(jnp.float32) for t in range(snaps)]
        keys = [qkv[t * size : (t + 1) * size, width : 2 * width].astype(jnp.float32) for t in range(snaps)]
        vals = [qkv[t * size : (t + 1) * size, 2 * width :].astype(jnp.float32) for t in range(snaps)]
        contexts = []
        for t in range(snaps):
            scores = []
            for u in range(t + 1):
                product = query[t] * keys[u]
                upper = product.astype(jnp.bfloat16)
                lower = (product - upper.astype(jnp.float32)).astype(jnp.bfloat16)
                total = matmul(upper, gather_heads) + matmul(lower, gather_heads)
                scores.append(total / math.sqrt(head))
            largest = functools.reduce(jnp.maximum, scores)
            expo = [jnp.exp(s - largest) for s in scores]
            total = functools.reduce(jnp.add, expo)
            context = None
            for u in range(t + 1):
                weight = matmul((expo[u] / total).astype(jnp.bfloat16), widen_heads)
                term = weight * vals[u]
                context = term if context is None else context + term
            contexts.append(context.astype(jnp.bfloat16))
        residual = mixed + matmul(jnp.concatenate(contexts, axis=0), wout_ref[...])
        normed_two = norm_rows(residual, gain2_ref[...].astype(jnp.float32)).astype(jnp.bfloat16)
        hidden = jax.nn.gelu(matmul(normed_two, up_ref[...])).astype(jnp.bfloat16)
        out = (residual + matmul(hidden, down_ref[...])).astype(out_ref.dtype)
        for t in range(snaps):
            out_ref[t, at] = out[t * size : (t + 1) * size]
        return carry

    lax.fori_loop(0, items // size, body, 0)


def per_device(
    features,
    tile_coord,
    tile_count,
    tile_values,
    w_agg,
    w_root,
    time_embed,
    gain_first,
    w_qkv,
    w_out,
    gain_second,
    w_up,
    w_down,
):
    own = features[0]
    pairs = tile_coord[0]
    tiles = tile_values[0]
    local, width = own.shape
    slots, tile = tiles.shape[0], tiles.shape[1]
    n_vertex = lax.axis_size("vertex")
    n_tm = lax.axis_size("tm")
    row_blocks = local // tile
    col_blocks = n_vertex * row_blocks
    chunk = 2 * tile
    chunks = local // chunk
    item = local // n_tm

    slot = jnp.arange(slots, dtype=jnp.int32)
    flat = jnp.where(slot < tile_count[0, 0], pairs[:, 0] * col_blocks + pairs[:, 1], -1)
    spot = jnp.arange(row_blocks * col_blocks, dtype=jnp.int32)
    table = jnp.min(jnp.where(flat[None, :] == spot[:, None], slot[None, :], slots), axis=1)

    anywhere = pl.BlockSpec(memory_space=pl.ANY)
    vmem = pl.BlockSpec(memory_space=pltpu.VMEM)
    landed = pl.pallas_call(
        functools.partial(graph_kernel, (n_vertex, n_tm, chunks, chunk, tile, slots)),
        out_shape=jax.ShapeDtypeStruct((n_tm, item, width), jnp.bfloat16),
        in_specs=[pl.BlockSpec(memory_space=pltpu.SMEM)] + [anywhere] * 4,
        out_specs=vmem,
        scratch_shapes=[
            pltpu.VMEM((n_vertex, local, width), jnp.bfloat16),
            pltpu.VMEM((slots + 1, tile, tile), jnp.bfloat16),
            pltpu.VMEM((width, width), jnp.bfloat16),
            pltpu.VMEM((width, width), jnp.bfloat16),
            pltpu.VMEM((local, width), jnp.float32),
            pltpu.VMEM((local, chunk), jnp.bfloat16),
            pltpu.VMEM((n_tm, item, width), jnp.bfloat16),
            pltpu.SemaphoreType.DMA((4,)),
            pltpu.SemaphoreType.DMA((3, n_vertex, chunks)),
            pltpu.SemaphoreType.DMA((n_vertex, chunks)),
            pltpu.SemaphoreType.DMA((n_tm,)),
            pltpu.SemaphoreType.DMA((n_tm,)),
        ],
        compiler_params=pltpu.CompilerParams(
            collective_id=0, has_side_effects=True, vmem_limit_bytes=44 * MIB
        ),
    )(table, own, tiles, w_agg, w_root)
    return pl.pallas_call(
        temporal_body,
        out_shape=jax.ShapeDtypeStruct((n_tm, item, width), jnp.bfloat16),
        in_specs=[vmem] * 8,
        out_specs=vmem,
        compiler_params=pltpu.CompilerParams(vmem_limit_bytes=44 * MIB),
    )(landed, time_embed, gain_first[None], w_qkv, w_out, gain_second[None], w_up, w_down)


def solution(mesh):
    return jax.shard_map(
        per_device,
        mesh=mesh,
        in_specs=(
            P("tm", "vertex", None),
            P("tm", "vertex", None),
            P("tm", "vertex"),
            P("tm", "vertex", None, None),
            P(),
            P(),
            P(),
            P(),
            P(),
            P(),
            P(),
            P(),
            P(),
        ),
        out_specs=P(None, ("vertex", "tm"), None),
        check_vma=False,
    )
```

profile of v0, /device:TPU:1, one launch (start us, length us, event | category | flops | bytes accessed | tf_op | source)
XLA Modules:
  0.0 108.7 jit_solution(17331952147841768050)
XLA Ops:
  0.0 0.0 copy-start.8
  0.7 0.8 compare_select_fusion
  1.4 0.1 select_reduce_fusion.table_ref
  1.6 0.7 broadcast_in_dim.28.gain1_ref
  2.3 0.7 broadcast_in_dim.29.gain2_ref
  2.9 0.0 copy-start
  3.0 2.2 %copy-done = bf16[1,128,128,128]{3,2,1,0:T(8,128)(2,1)S(1)} copy-done((bf16[1,128,128,128]{3,2,1,0:T(8,128)(2,1)S(1)}, bf16[1,128,128,128]{3,2,1,0:T(8,128)(2,1)}, u32[]{:S(2)}) %copy-start) | copy-done | bytes 4194328
  5.1 0.0 copy-start.2
  5.1 1.2 %copy-done.2 = bf16[1,1024,512]{2,1,0:T(8,128)(2,1)S(1)} copy-done((bf16[1,1024,512]{2,1,0:T(8,128)(2,1)S(1)}, bf16[1,1024,512]{2,1,0:T(8,128)(2,1)}, u32[]{:S(2)}) %copy-start.2) | copy-done | bytes 1048600
  6.4 0.0 copy-start.6
  6.4 1.0 copy-done.6
  7.4 0.0 copy-start.7
  7.4 1.0 copy-done.7
  8.4 0.0 copy-start.1
  8.4 0.0 copy-start.3
  8.5 0.0 copy-start.4
  8.5 0.0 copy-start.5
  8.5 90.0 %shard_map.127.rows_ref = bf16[4,256,512]{2,1,0:T(8,128)(2,1)S(1)} custom-call(s32[512]{0:T(512)S(1)} %select_reduce_fusion.table_ref, bf16[1024,512]{1,0:T(8,128)(2,1)S(1)} %bitcast.8, bf16[128,128,128]{2,1,0:T(8,128)(2,1)S(1)} %bitcast.7, bf16[512,512]{1,0:T(8,128)(2,1)S(1)} %copy-done.6, bf16[512,512]{1,0:T(8,128)(2,1)S(1)} %copy-done.7), custom_call_target="tpu_custom_call" | custom-call | tf_op jit(solution)/shard_map/pallas_call | solution.py:358
  98.5 0.0 copy-done.8
  98.5 0.0 copy-done.1
  98.5 0.0 copy-done.3
  98.5 0.0 copy-done.4
  98.5 0.0 copy-done.5
  98.5 10.2 %shard_map.128 = bf16[4,256,512]{2,1,0:T(8,128)(2,1)} custom-call(bf16[4,256,512]{2,1,0:T(8,128)(2,1)S(1)} %shard_map.127.rows_ref, bf16[4,512]{1,0:T(4,128)(2,1)S(1)} %copy-done.8, bf16[1,512]{1,0:T(2,128)(2,1)S(1)} %broadcast_in_dim.28.gain1_ref, bf16[512,1536]{1,0:T(8,128)(2,1)S(1)} %copy-done.1, bf16[512,512]{1,0:T(8,128)(2,1)S(1)} %copy-done.5, ...), custom_call_target="tpu_custom_call" | custom-call | tf_op jit(solution)/shard_map/pallas_call | solution.py:381
Async XLA Ops:
  0.0 98.5 %copy-start.8 = (bf16[4,512]{1,0:T(4,128)(2,1)S(1)}, bf16[4,512]{1,0:T(4,128)(2,1)}, u32[]{:S(2)}) copy-start(bf16[4,512]{1,0:T(4,128)(2,1)} %embed_ref.1) | copy-start | bytes 12292
  2.9 2.2 %copy-start = (bf16[1,128,128,128]{3,2,1,0:T(8,128)(2,1)S(1)}, bf16[1,128,128,128]{3,2,1,0:T(8,128)(2,1)}, u32[]{:S(2)}) copy-start(bf16[1,128,128,128]{3,2,1,0:T(8,128)(2,1)} %param.16) | copy-start | bytes 12582916
  5.1 1.2 %copy-start.2 = (bf16[1,1024,512]{2,1,0:T(8,128)(2,1)S(1)}, bf16[1,1024,512]{2,1,0:T(8,128)(2,1)}, u32[]{:S(2)}) copy-start(bf16[1,1024,512]{2,1,0:T(8,128)(2,1)} %param.13) | copy-start | bytes 3145732
  6.4 1.0 copy-start.6
  7.4 1.0 copy-start.7
  8.4 90.0 %copy-start.1 = (bf16[512,1536]{1,0:T(8,128)(2,1)S(1)}, bf16[512,1536]{1,0:T(8,128)(2,1)}, u32[]{:S(2)}) copy-start(bf16[512,1536]{1,0:T(8,128)(2,1)} %qkv_ref.1) | copy-start | bytes 4718596
  8.4 90.0 %copy-start.3 = (bf16[512,1024]{1,0:T(8,128)(2,1)S(1)}, bf16[512,1024]{1,0:T(8,128)(2,1)}, u32[]{:S(2)}) copy-start(bf16[512,1024]{1,0:T(8,128)(2,1)} %up_ref.1) | copy-start | bytes 3145732
  8.5 90.0 %copy-start.4 = (bf16[1024,512]{1,0:T(8,128)(2,1)S(1)}, bf16[1024,512]{1,0:T(8,128)(2,1)}, u32[]{:S(2)}) copy-start(bf16[1024,512]{1,0:T(8,128)(2,1)} %down_ref.1) | copy-start | bytes 3145732
  8.5 90.0 %copy-start.5 = (bf16[512,512]{1,0:T(8,128)(2,1)S(1)}, bf16[512,512]{1,0:T(8,128)(2,1)}, u32[]{:S(2)}) copy-start(bf16[512,512]{1,0:T(8,128)(2,1)} %wout_ref.1) | copy-start | bytes 1572868
where the time goes:
time: 109 us
  Pallas kernels  100 us (92%)
  local copies, waits for them, and re-layouts  6.88 us (6%)
    pallas_call x1, Pallas kernels, per_device(): pl.pallas_call(functools.partial(graph_kernel, (n_vertex, n_tm, chunks, c...  90 us
    pallas_call x1, Pallas kernels, per_device(): pl.pallas_call(temporal_body, out_shape=jax.ShapeDtypeStruct((n_tm, item,...  10.2 us
    unnamed x18, local copies, waits for them, and re-layouts  5.51 us

commit v1 on v0

--- a/solution.py
+++ b/solution.py
@@ -21,21 +21,34 @@
     tiles_ref,
     wagg_ref,
     wroot_ref,
-    land_ref,
+    qkv_ref,
+    wout_ref,
+    up_ref,
+    down_ref,
+    embed_ref,
+    gain1_ref,
+    gain2_ref,
+    out_ref,
     xbuf,
     tiles_v,
     wagg_v,
     wroot_v,
+    qkv_v,
+    wout_v,
+    up_v,
+    down_v,
     acc,
+    root,
     a_buf,
     stage,
+    land,
     local_sem,
     send_sem,
     recv_sem,
     a2a_send,
     a2a_recv,
 ):
-    n_vertex, n_tm, chunks, chunk, tile, slots = cfg
+    n_vertex, n_tm, chunks, chunk, tile, slots, sub = cfg
     chips = n_vertex // CORES
     local = feat_ref.shape[0]
     row_blocks = local // tile
@@ -72,10 +85,13 @@
     tile_copy = pltpu.make_async_copy(tiles_ref, tiles_v.at[pl.ds(0, slots)], local_sem.at[1])
     agg_copy = pltpu.make_async_copy(wagg_ref, wagg_v, local_sem.at[2])
     root_copy = pltpu.make_async_copy(wroot_ref, wroot_v, local_sem.at[3])
+    weight_copies = [
+        pltpu.make_async_copy(source, target, local_sem.at[4 + i])
+        for i, (source, target) in enumerate(
+            [(qkv_ref, qkv_v), (wout_ref, wout_v), (up_ref, up_v), (down_ref, down_v)]
+        )
+    ]
     own_copy.start()
-    tile_copy.start()
-    agg_copy.start()
-    root_copy.start()
 
     ends = jnp.where(has_right, 1, 0) + jnp.where(has_left, 1, 0)
     pl.semaphore_wait(barrier, n_tm + ends)
@@ -132,11 +148,13 @@
         return carry
 
     lax.fori_loop(0, chunks, send_own, 0)
+    for copy in [tile_copy, root_copy, agg_copy] + weight_copies:
+        copy.start()
     tiles_v[slots] = jnp.zeros(tiles_v.shape[1:], tiles_v.dtype)
     acc[...] = jnp.zeros_like(acc)
-    tile_copy.wait()
-    agg_copy.wait()
-    root_copy.wait()
+    for copy in [tile_copy, root_copy, agg_copy] + weight_copies:
+        copy.wait()
+    root[...] = jnp.dot(xbuf[me], wroot_v[...], preferred_element_type=jnp.float32)
 
     def first_step(i, carry):
         part = lax.rem(i, chunks)
@@ -191,42 +209,60 @@
 
     lax.fori_loop(0, (chips - 1) * chunks, step, 0)
 
-    def block(i, carry):
-        to = lax.rem(tm + i, n_tm)
-        rows = pl.ds(pl.multiple_of(to * item, item), item)
-        neighbor_sum = acc[rows].astype(jnp.bfloat16)
-        combined = jnp.dot(neighbor_sum, wagg_v[...], preferred_element_type=jnp.float32)
-        combined += jnp.dot(xbuf[me, rows], wroot_v[...], preferred_element_type=jnp.float32)
-        stage[to] = jax.nn.gelu(combined).astype(jnp.bfloat16)
-
-        @pl.when(i < n_tm)
-        def _():
-            trade(to).start()
-
-        return carry
-
-    def trade(to):
+    def trade(to, part):
+        rows = pl.ds(pl.multiple_of(part * sub, sub), sub)
         return pltpu.make_async_remote_copy(
-            src_ref=stage.at[to],
-            dst_ref=land_ref.at[tm],
-            send_sem=a2a_send.at[to],
-            recv_sem=a2a_recv.at[tm],
+            src_ref=stage.at[to, rows],
+            dst_ref=land.at[tm, rows],
+            send_sem=a2a_send.at[to, part],
+            recv_sem=a2a_recv.at[tm, part],
             device_id={"tm": to},
             device_id_type=MESH,
         )
 
-    def landed(source):
+    def landed(source, part):
+        rows = pl.ds(pl.multiple_of(part * sub, sub), sub)
         return pltpu.make_async_remote_copy(
-            src_ref=stage.at[source],
-            dst_ref=land_ref.at[source],
-            send_sem=a2a_send.at[source],
-            recv_sem=a2a_recv.at[source],
+            src_ref=stage.at[source, rows],
+            dst_ref=land.at[source, rows],
+            send_sem=a2a_send.at[source, part],
+            recv_sem=a2a_recv.at[source, part],
             device_id={"tm": source},
             device_id_type=MESH,
         )
 
-    lax.fori_loop(1, n_tm + 1, block, 0)
-    land_ref[tm] = stage[tm]
+    def block(part, carry):
+        def rows_of(to):
+            return pl.ds(pl.multiple_of(to * item + part * sub, sub), sub)
+
+        here = pl.ds(pl.multiple_of(part * sub, sub), sub)
+        summed = jnp.concatenate([acc[rows_of(to)] for to in range(n_tm)], axis=0)
+        based = jnp.concatenate([root[rows_of(to)] for to in range(n_tm)], axis=0)
+        combined = based + matmul(summed.astype(jnp.bfloat16), wagg_v[...])
+        graph_rows = jax.nn.gelu(combined).astype(jnp.bfloat16)
+        for to in range(n_tm):
+            stage[to, here] = graph_rows[to * sub : (to + 1) * sub]
+
+        def send(i, inner):
+            trade(lax.rem(tm + i, n_tm), part).start()
+            return inner
+
+        lax.fori_loop(1, n_tm, send, 0)
+        land[tm, here] = stage[tm, here]
+        return carry
+
+    lax.fori_loop(0, item // sub, block, 0)
+
+    def await_rows(part):
+        def one(i, inner):
+            landed(lax.rem(tm + i, n_tm), part).wait_recv()
+            return inner
+
+        lax.fori_loop(1, n_tm, one, 0)
+
+    temporal_body(
+        await_rows, sub, land, embed_ref, gain1_ref, qkv_v, wout_v, gain2_ref, up_v, down_v, out_ref
+    )
 
     def settle_own(part, carry):
         settle(me, part, has_right, has_left)
@@ -253,12 +289,10 @@
     lax.fori_loop(0, (chips - 1) * chunks, settle_step, 0)
 
     def finish(i, carry):
-        partner = lax.rem(tm + i, n_tm)
-        trade(partner).wait_send()
-        landed(partner).wait_recv()
-        return carry
-
-    lax.fori_loop(1, n_tm, finish, 0)
+        trade(lax.rem(tm + 1 + i // (item // sub), n_tm), lax.rem(i, item // sub)).wait_send()
+        return carry
+
+    lax.fori_loop(0, (n_tm - 1) * (item // sub), finish, 0)
 
 
 def norm_rows(values, gain):
@@ -270,23 +304,25 @@
     return jnp.dot(left, right, preferred_element_type=jnp.float32)
 
 
-def temporal_body(rows_ref, embed_ref, gain1_ref, qkv_ref, wout_ref, gain2_ref, up_ref, down_ref, out_ref):
+def temporal_body(
+    await_rows, size, rows_ref, embed_ref, gain1_ref, qkv_ref, wout_ref, gain2_ref, up_ref, down_ref, out_ref
+):
     snaps, items, width = rows_ref.shape
     head = width // HEADS
     lanes = 128
-    size = max(16, min(items, 512 // snaps))
     col_head = lax.broadcasted_iota(jnp.int32, (width, lanes), 0) // head
     gather_heads = (col_head == lax.broadcasted_iota(jnp.int32, (width, lanes), 1)).astype(jnp.bfloat16)
     row_head = lax.broadcasted_iota(jnp.int32, (lanes, width), 1) // head
     widen_heads = (row_head == lax.broadcasted_iota(jnp.int32, (lanes, width), 0)).astype(jnp.bfloat16)
 
     def body(i, carry):
+        await_rows(i)
         at = pl.ds(pl.multiple_of(i * size, size), size)
         embed = embed_ref[...].astype(jnp.float32)
         mixed = jnp.concatenate(
             [rows_ref[t, at].astype(jnp.float32) + embed[t : t + 1] for t in range(snaps)], axis=0
         )
-        normed = norm_rows(mixed, gain1_ref[...].astype(jnp.float32)).astype(jnp.bfloat16)
+        normed = norm_rows(mixed, gain1_ref[...].astype(jnp.float32)[None]).astype(jnp.bfloat16)
         qkv = matmul(normed, qkv_ref[...]).astype(jnp.bfloat16)
         query = [qkv[t * size : (t + 1) * size, :width].astype(jnp.float32) for t in range(snaps)]
         keys = [qkv[t * size : (t + 1) * size, width : 2 * width].astype(jnp.float32) for t in range(snaps)]
@@ -310,7 +346,7 @@
                 context = term if context is None else context + term
             contexts.append(context.astype(jnp.bfloat16))
         residual = mixed + matmul(jnp.concatenate(contexts, axis=0), wout_ref[...])
-        normed_two = norm_rows(residual, gain2_ref[...].astype(jnp.float32)).astype(jnp.bfloat16)
+        normed_two = norm_rows(residual, gain2_ref[...].astype(jnp.float32)[None]).astype(jnp.bfloat16)
         hidden = jax.nn.gelu(matmul(normed_two, up_ref[...])).astype(jnp.bfloat16)
         out = (residual + matmul(hidden, down_ref[...])).astype(out_ref.dtype)
         for t in range(snaps):
@@ -347,6 +383,7 @@
     chunk = 2 * tile
     chunks = local // chunk
     item = local // n_tm
+    sub = max(16, min(item, 256 // n_tm))
 
     slot = jnp.arange(slots, dtype=jnp.int32)
     flat = jnp.where(slot < tile_count[0, 0], pairs[:, 0] * col_blocks + pairs[:, 1], -1)
@@ -355,36 +392,35 @@
 
     anywhere = pl.BlockSpec(memory_space=pl.ANY)
     vmem = pl.BlockSpec(memory_space=pltpu.VMEM)
-    landed = pl.pallas_call(
-        functools.partial(graph_kernel, (n_vertex, n_tm, chunks, chunk, tile, slots)),
+    return pl.pallas_call(
+        functools.partial(graph_kernel, (n_vertex, n_tm, chunks, chunk, tile, slots, sub)),
         out_shape=jax.ShapeDtypeStruct((n_tm, item, width), jnp.bfloat16),
-        in_specs=[pl.BlockSpec(memory_space=pltpu.SMEM)] + [anywhere] * 4,
+        in_specs=[pl.BlockSpec(memory_space=pltpu.SMEM)] + [anywhere] * 8 + [vmem] * 3,
         out_specs=vmem,
         scratch_shapes=[
             pltpu.VMEM((n_vertex, local, width), jnp.bfloat16),
             pltpu.VMEM((slots + 1, tile, tile), jnp.bfloat16),
-            pltpu.VMEM((width, width), jnp.bfloat16),
-            pltpu.VMEM((width, width), jnp.bfloat16),
+            pltpu.VMEM(w_agg.shape, jnp.bfloat16),
+            pltpu.VMEM(w_root.shape, jnp.bfloat16),
+            pltpu.VMEM(w_qkv.shape, jnp.bfloat16),
+            pltpu.VMEM(w_out.shape, jnp.bfloat16),
+            pltpu.VMEM(w_up.shape, jnp.bfloat16),
+            pltpu.VMEM(w_down.shape, jnp.bfloat16),
+            pltpu.VMEM((local, width), jnp.float32),
             pltpu.VMEM((local, width), jnp.float32),
             pltpu.VMEM((local, chunk), jnp.bfloat16),
             pltpu.VMEM((n_tm, item, width), jnp.bfloat16),
-            pltpu.SemaphoreType.DMA((4,)),
+            pltpu.VMEM((n_tm, item, width), jnp.bfloat16),
+            pltpu.SemaphoreType.DMA((8,)),
             pltpu.SemaphoreType.DMA((3, n_vertex, chunks)),
             pltpu.SemaphoreType.DMA((n_vertex, chunks)),
-            pltpu.SemaphoreType.DMA((n_tm,)),
-            pltpu.SemaphoreType.DMA((n_tm,)),
+            pltpu.SemaphoreType.DMA((n_tm, item // sub)),
+            pltpu.SemaphoreType.DMA((n_tm, item // sub)),
         ],
         compiler_params=pltpu.CompilerParams(
-            collective_id=0, has_side_effects=True, vmem_limit_bytes=44 * MIB
+            collective_id=0, has_side_effects=True, vmem_limit_bytes=56 * MIB
         ),
-    )(table, own, tiles, w_agg, w_root)
-    return pl.pallas_call(
-        temporal_body,
-        out_shape=jax.ShapeDtypeStruct((n_tm, item, width), jnp.bfloat16),
-        in_specs=[vmem] * 8,
-        out_specs=vmem,
-        compiler_params=pltpu.CompilerParams(vmem_limit_bytes=44 * MIB),
-    )(landed, time_embed, gain_first[None], w_qkv, w_out, gain_second[None], w_up, w_down)
+    )(table, own, tiles, w_agg, w_root, w_qkv, w_out, w_up, w_down, time_embed, gain_first, gain_second)
 
 
 def solution(mesh):

time: 109 us -> 99.8 us (0.916)
  Pallas kernels: 100 us -> 95.2 us
  local copies, waits for them, and re-layouts: 6.88 us -> 2.26 us
    pallas_call x1 -> x0, Pallas kernels: 10.2 us -> none  [per_device(): pl.pallas_call(temporal_body, out_shape=jax.ShapeDtypeStruct((n_tm, item,...]
    pallas_call x1, Pallas kernels: 90 us -> 95.2 us  [per_device(): pl.pallas_call(functools.partial(graph_kernel, (n_vertex, n_tm, chunks, c...]
    unnamed x18 -> x1, local copies, waits for them, and re-layouts: 5.51 us -> 2.26 us
    broadcast_in_dim x2 -> x0, local copies, waits for them, and re-layouts: 1.37 us -> none  [the longest x1 0.68 us: per_device(): gain_first[None]]
where the time goes in v1:
time: 99.8 us; the launch traced here: 99.6 us
  Pallas kernels  95.2 us (95%)
  local copies, waits for them, and re-layouts  2.26 us (2%)
  other arithmetic  1.49 us (1%)
    pallas_call x1, Pallas kernels, per_device(): pl.pallas_call(functools.partial(graph_kernel, (n_vertex, n_tm, chunks, c...  95.2 us
    unnamed x1, local copies, waits for them, and re-layouts  2.26 us

profile of v1, /device:TPU:1, one launch (start us, length us, event | category | flops | bytes accessed | tf_op | source)
XLA Modules:
  0.0 99.6 jit_solution(12844359104656856716)
XLA Ops:
  0.7 0.8 compare_select_fusion
  1.4 0.7 select_reduce_fusion.table_ref
  2.1 95.2 %shard_map.127 = bf16[4,256,512]{2,1,0:T(8,128)(2,1)} custom-call(s32[512]{0:T(512)} %select_reduce_fusion.table_ref, bf16[1024,512]{1,0:T(8,128)(2,1)} %bitcast.8, bf16[128,128,128]{2,1,0:T(8,128)(2,1)} %bitcast.7, bf16[512,512]{1,0:T(8,128)(2,1)} %wagg_ref.1, bf16[512,512]{1,0:T(8,128)(2,1)} %wroot_ref.1, bf16[512,1536]{1,0:T(8,128)(2,1)} %qkv_ref.1, ...), custom_call_target="tpu_custom_call" | custom-call | tf_op jit(solution)/shard_map/pallas_call | solution.py:395
  97.3 2.3 %copy.16 = bf16[4,256,512]{2,1,0:T(8,128)(2,1)} copy(bf16[4,256,512]{2,1,0:T(8,128)(2,1)} %shard_map.127) | data formatting | bytes 2097152

commit v2 on v1

--- a/solution.py
+++ b/solution.py
@@ -12,11 +12,25 @@
 CORES = 2
 MESH = pl.DeviceIdType.MESH
 MIB = 1 << 20
+LANES = 128
+
+
+def fill_table(live, pairs_ref, table_ref, slots, col_blocks):
+    lane = lax.broadcasted_iota(jnp.int32, (1, slots), 1)
+    flat = pairs_ref[0:1] * col_blocks + pairs_ref[1:2]
+    flat = jnp.where(lane < live, flat, -1)
+    wide = jnp.broadcast_to(flat, (LANES, slots)).T
+    slot = lax.broadcasted_iota(jnp.int32, (slots, LANES), 0)
+    column = lax.broadcasted_iota(jnp.int32, (slots, LANES), 1)
+    for row in range(table_ref.shape[0]):
+        hit = jnp.where(wide == column + row * LANES, slot, slots)
+        table_ref[row : row + 1] = jnp.min(hit, axis=0, keepdims=True)
 
 
 def graph_kernel(
     cfg,
-    table_ref,
+    count_ref,
+    pairs_ref,
     feat_ref,
     tiles_ref,
     wagg_ref,
@@ -42,6 +56,8 @@
     a_buf,
     stage,
     land,
+    table_v,
+    table_s,
     local_sem,
     send_sem,
     recv_sem,
@@ -136,7 +152,8 @@
         first = shard * row_blocks + part * per_chunk
         for r in range(row_blocks):
             for j in range(per_chunk):
-                slot = table_ref[r * col_blocks + first + j]
+                spot = r * col_blocks + first + j
+                slot = table_s[spot // LANES, lax.rem(spot, LANES)]
                 a_buf[r * tile : (r + 1) * tile, j * tile : (j + 1) * tile] = tiles_v[slot]
         rows = pl.ds(pl.multiple_of(part * chunk, chunk), chunk)
         acc[...] += jnp.dot(a_buf[...], xbuf[shard, rows], preferred_element_type=jnp.float32)
@@ -150,10 +167,14 @@
     lax.fori_loop(0, chunks, send_own, 0)
     for copy in [tile_copy, root_copy, agg_copy] + weight_copies:
         copy.start()
+    fill_table(count_ref[0, 0], pairs_ref, table_v, slots, col_blocks)
+    table_copy = pltpu.make_async_copy(table_v, table_s, local_sem.at[8])
+    table_copy.start()
     tiles_v[slots] = jnp.zeros(tiles_v.shape[1:], tiles_v.dtype)
     acc[...] = jnp.zeros_like(acc)
     for copy in [tile_copy, root_copy, agg_copy] + weight_copies:
         copy.wait()
+    table_copy.wait()
     root[...] = jnp.dot(xbuf[me], wroot_v[...], preferred_element_type=jnp.float32)
 
     def first_step(i, carry):
@@ -327,24 +348,30 @@
         query = [qkv[t * size : (t + 1) * size, :width].astype(jnp.float32) for t in range(snaps)]
         keys = [qkv[t * size : (t + 1) * size, width : 2 * width].astype(jnp.float32) for t in range(snaps)]
         vals = [qkv[t * size : (t + 1) * size, 2 * width :].astype(jnp.float32) for t in range(snaps)]
-        contexts = []
+        uppers, lowers = [], []
         for t in range(snaps):
-            scores = []
             for u in range(t + 1):
                 product = query[t] * keys[u]
                 upper = product.astype(jnp.bfloat16)
-                lower = (product - upper.astype(jnp.float32)).astype(jnp.bfloat16)
-                total = matmul(upper, gather_heads) + matmul(lower, gather_heads)
-                scores.append(total / math.sqrt(head))
+                uppers.append(upper)
+                lowers.append((product - upper.astype(jnp.float32)).astype(jnp.bfloat16))
+        totals = matmul(jnp.concatenate(uppers + lowers, axis=0), gather_heads)
+        count = len(uppers) * size
+        all_scores = (totals[:count] + totals[count:]) / math.sqrt(head)
+        weights = []
+        for t in range(snaps):
+            first = t * (t + 1) // 2
+            scores = [all_scores[(first + u) * size : (first + u + 1) * size] for u in range(t + 1)]
             largest = functools.reduce(jnp.maximum, scores)
-            expo = [jnp.exp(s - largest) for s in scores]
+            expo = [jnp.exp(score - largest) for score in scores]
             total = functools.reduce(jnp.add, expo)
-            context = None
-            for u in range(t + 1):
-                weight = matmul((expo[u] / total).astype(jnp.bfloat16), widen_heads)
-                term = weight * vals[u]
-                context = term if context is None else context + term
-            contexts.append(context.astype(jnp.bfloat16))
+            weights += [(each / total).astype(jnp.bfloat16) for each in expo]
+        wide = matmul(jnp.concatenate(weights, axis=0), widen_heads)
+        contexts = []
+        for t in range(snaps):
+            first = t * (t + 1) // 2
+            terms = [wide[(first + u) * size : (first + u + 1) * size] * vals[u] for u in range(t + 1)]
+            contexts.append(functools.reduce(jnp.add, terms).astype(jnp.bfloat16))
         residual = mixed + matmul(jnp.concatenate(contexts, axis=0), wout_ref[...])
         normed_two = norm_rows(residual, gain2_ref[...].astype(jnp.float32)[None]).astype(jnp.bfloat16)
         hidden = jax.nn.gelu(matmul(normed_two, up_ref[...])).astype(jnp.bfloat16)
@@ -385,17 +412,12 @@
     item = local // n_tm
     sub = max(16, min(item, 256 // n_tm))
 
-    slot = jnp.arange(slots, dtype=jnp.int32)
-    flat = jnp.where(slot < tile_count[0, 0], pairs[:, 0] * col_blocks + pairs[:, 1], -1)
-    spot = jnp.arange(row_blocks * col_blocks, dtype=jnp.int32)
-    table = jnp.min(jnp.where(flat[None, :] == spot[:, None], slot[None, :], slots), axis=1)
-
     anywhere = pl.BlockSpec(memory_space=pl.ANY)
     vmem = pl.BlockSpec(memory_space=pltpu.VMEM)
     return pl.pallas_call(
         functools.partial(graph_kernel, (n_vertex, n_tm, chunks, chunk, tile, slots, sub)),
         out_shape=jax.ShapeDtypeStruct((n_tm, item, width), jnp.bfloat16),
-        in_specs=[pl.BlockSpec(memory_space=pltpu.SMEM)] + [anywhere] * 8 + [vmem] * 3,
+        in_specs=[pl.BlockSpec(memory_space=pltpu.SMEM), vmem] + [anywhere] * 8 + [vmem] * 3,
         out_specs=vmem,
         scratch_shapes=[
             pltpu.VMEM((n_vertex, local, width), jnp.bfloat16),
@@ -411,7 +433,9 @@
             pltpu.VMEM((local, chunk), jnp.bfloat16),
             pltpu.VMEM((n_tm, item, width), jnp.bfloat16),
             pltpu.VMEM((n_tm, item, width), jnp.bfloat16),
-            pltpu.SemaphoreType.DMA((8,)),
+            pltpu.VMEM((row_blocks * col_blocks // LANES, LANES), jnp.int32),
+            pltpu.SMEM((row_blocks * col_blocks // LANES, LANES), jnp.int32),
+            pltpu.SemaphoreType.DMA((9,)),
             pltpu.SemaphoreType.DMA((3, n_vertex, chunks)),
             pltpu.SemaphoreType.DMA((n_vertex, chunks)),
             pltpu.SemaphoreType.DMA((n_tm, item // sub)),
@@ -420,7 +444,7 @@
         compiler_params=pltpu.CompilerParams(
             collective_id=0, has_side_effects=True, vmem_limit_bytes=56 * MIB
         ),
-    )(table, own, tiles, w_agg, w_root, w_qkv, w_out, w_up, w_down, time_embed, gain_first, gain_second)
+    )(tile_count, pairs.T, own, tiles, w_agg, w_root, w_qkv, w_out, w_up, w_down, time_embed, gain_first, gain_second)
 
 
 def solution(mesh):

time: 99.8 us -> 97.8 us (0.980)
  other arithmetic: 1.49 us -> 0 us
where the time goes in v2:
time: 97.8 us; the launch traced here: 97.6 us
  Pallas kernels  94.6 us (97%)
  local copies, waits for them, and re-layouts  2.26 us (2%)
    pallas_call x1, Pallas kernels, per_device(): pl.pallas_call(functools.partial(graph_kernel, (n_vertex, n_tm, chunks, c...  94.6 us
    unnamed x1, local copies, waits for them, and re-layouts  2.26 us

profile of v2, /device:TPU:1, one launch (start us, length us, event | category | flops | bytes accessed | tf_op | source)
XLA Modules:
  0.0 97.6 jit_solution(8314841150570031968)
XLA Ops:
  0.7 94.6 %shard_map.127 = bf16[4,256,512]{2,1,0:T(8,128)(2,1)} custom-call(s32[1,1]{1,0:T(1,128)S(6)} %copy.15.count_ref, s32[2,128]{1,0:T(2,128)} %bitcast.7, bf16[1024,512]{1,0:T(8,128)(2,1)} %bitcast.6, bf16[128,128,128]{2,1,0:T(8,128)(2,1)} %bitcast.5, bf16[512,512]{1,0:T(8,128)(2,1)} %wagg_ref.1, bf16[512,512]{1,0:T(8,128)(2,1)} %wroot_ref.1, ...), custom_call_target="tpu_custom_call" | custom-call | tf_op jit(solution)/shard_map/pallas_call | solution.py:417
  95.3 2.3 %copy.16 = bf16[4,256,512]{2,1,0:T(8,128)(2,1)} copy(bf16[4,256,512]{2,1,0:T(8,128)(2,1)} %shard_map.127) | data formatting | bytes 2097152

commit v3 on v2

--- a/solution.py
+++ b/solution.py
@@ -56,6 +56,8 @@
     a_buf,
     stage,
     land,
+    out_v,
+    out_sem,
     table_v,
     table_s,
     local_sem,
@@ -281,8 +283,15 @@
 
         lax.fori_loop(1, n_tm, one, 0)
 
+    def hand_over(part):
+        rows = pl.ds(pl.multiple_of(part * sub, sub), sub)
+        return pltpu.make_async_copy(out_v.at[:, rows], out_ref.at[:, rows], out_sem.at[part])
+
+    def hand_out(part):
+        hand_over(part).start()
+
     temporal_body(
-        await_rows, sub, land, embed_ref, gain1_ref, qkv_v, wout_v, gain2_ref, up_v, down_v, out_ref
+        await_rows, sub, land, embed_ref, gain1_ref, qkv_v, wout_v, gain2_ref, up_v, down_v, out_v, hand_out
     )
 
     def settle_own(part, carry):
@@ -315,6 +324,12 @@
 
     lax.fori_loop(0, (n_tm - 1) * (item // sub), finish, 0)
 
+    def handed(part, carry):
+        hand_over(part).wait()
+        return carry
+
+    lax.fori_loop(0, item // sub, handed, 0)
+
 
 def norm_rows(values, gain):
     scale = lax.rsqrt(jnp.mean(values * values, axis=-1, keepdims=True) + 1e-06)
@@ -326,7 +341,7 @@
 
 
 def temporal_body(
-    await_rows, size, rows_ref, embed_ref, gain1_ref, qkv_ref, wout_ref, gain2_ref, up_ref, down_ref, out_ref
+    await_rows, size, rows_ref, embed_ref, gain1_ref, qkv_ref, wout_ref, gain2_ref, up_ref, down_ref, out_ref, hand_out
 ):
     snaps, items, width = rows_ref.shape
     head = width // HEADS
@@ -378,6 +393,7 @@
         out = (residual + matmul(hidden, down_ref[...])).astype(out_ref.dtype)
         for t in range(snaps):
             out_ref[t, at] = out[t * size : (t + 1) * size]
+        hand_out(i)
         return carry
 
     lax.fori_loop(0, items // size, body, 0)
@@ -418,7 +434,7 @@
         functools.partial(graph_kernel, (n_vertex, n_tm, chunks, chunk, tile, slots, sub)),
         out_shape=jax.ShapeDtypeStruct((n_tm, item, width), jnp.bfloat16),
         in_specs=[pl.BlockSpec(memory_space=pltpu.SMEM), vmem] + [anywhere] * 8 + [vmem] * 3,
-        out_specs=vmem,
+        out_specs=anywhere,
         scratch_shapes=[
             pltpu.VMEM((n_vertex, local, width), jnp.bfloat16),
             pltpu.VMEM((slots + 1, tile, tile), jnp.bfloat16),
@@ -433,6 +449,8 @@
             pltpu.VMEM((local, chunk), jnp.bfloat16),
             pltpu.VMEM((n_tm, item, width), jnp.bfloat16),
             pltpu.VMEM((n_tm, item, width), jnp.bfloat16),
+            pltpu.VMEM((n_tm, item, width), jnp.bfloat16),
+            pltpu.SemaphoreType.DMA((item // sub,)),
             pltpu.VMEM((row_blocks * col_blocks // LANES, LANES), jnp.int32),
             pltpu.SMEM((row_blocks * col_blocks // LANES, LANES), jnp.int32),
             pltpu.SemaphoreType.DMA((9,)),

time: 97.8 us -> 97 us (level)
  no operation moved by 1% of the time
where the time goes in v3:
time: 97 us; the launch traced here: 96.8 us
  Pallas kernels  93.9 us (97%)
  local copies, waits for them, and re-layouts  2.26 us (2%)
    pallas_call x1, Pallas kernels, per_device(): pl.pallas_call(functools.partial(graph_kernel, (n_vertex, n_tm, chunks, c...  93.9 us
    unnamed x1, local copies, waits for them, and re-layouts  2.26 us

profile of v3, /device:TPU:1, one launch (start us, length us, event | category | flops | bytes accessed | tf_op | source)
XLA Modules:
  0.0 96.8 jit_solution(12473705066340691528)
XLA Ops:
  0.7 93.9 %shard_map.127 = bf16[4,256,512]{2,1,0:T(8,128)(2,1)} custom-call(s32[1,1]{1,0:T(1,128)S(6)} %copy.15.count_ref, s32[2,128]{1,0:T(2,128)} %bitcast.7, bf16[1024,512]{1,0:T(8,128)(2,1)} %bitcast.6, bf16[128,128,128]{2,1,0:T(8,128)(2,1)} %bitcast.5, bf16[512,512]{1,0:T(8,128)(2,1)} %wagg_ref.1, bf16[512,512]{1,0:T(8,128)(2,1)} %wroot_ref.1, ...), custom_call_target="tpu_custom_call" | custom-call | tf_op jit(solution)/shard_map/pallas_call | solution.py:433
  94.5 2.3 %copy.16 = bf16[4,256,512]{2,1,0:T(8,128)(2,1)} copy(bf16[4,256,512]{2,1,0:T(8,128)(2,1)} %shard_map.127) | data formatting | bytes 2097152
